TPU v7x, 32 devices: a whole 2x2x4 slice. The times are simulated.
32 devices in a mesh: frames: 8 (over y, x, core), rows: 4 (over z).
Axes of the slice: x: 2, y: 2, z: 4, core: 2. Of those that a mesh axis runs over, the one named last changes fastest.
Arguments:
- input_feature_maps: float32 [96, 16, 16, 1024], P('frames', 'rows'), may hold values from -6 to 6
- sequence_slot_lookup: int32 [96], P('frames'), may hold values from 0 to 31, as said below
- sequence_span_lookup: int32 [96], P('frames'), may hold values from 8 to 32, as said below
- opening_reducer: bfloat16 [1024, 512], replicated, may hold values from -0.1875 to 0.1875
- downsampling_filter: bfloat16 [3, 3, 512, 512], replicated, may hold values from -0.09375 to 0.09375
- opening_expander: bfloat16 [512, 2048], replicated, may hold values from -0.25 to 0.25
- skip_projection: bfloat16 [1024, 2048], replicated, may hold values from -0.1875 to 0.1875
- closing_reducer: bfloat16 [2048, 512], replicated, may hold values from -0.125 to 0.125
- excite_reducer: bfloat16 [512, 32], replicated, may hold values from -0.25 to 0.25
- excite_spatial_filter: bfloat16 [3, 3, 32, 32], replicated, may hold values from -0.375 to 0.375
- excite_expander: bfloat16 [32, 512], replicated, may hold values from -4 to 4
- time_taps: bfloat16 [3, 384], replicated, may hold values from 0.19921875 to 0.796875
- spatial_filters: bfloat16 [3, 3, 3, 128, 128], replicated, may hold values from -0.1875 to 0.1875
- closing_expander: bfloat16 [512, 2048], replicated, may hold values from -0.25 to 0.25
- narrow_norm_gains: float32 [4, 512], replicated, may hold values from 0.5 to 1.5
- narrow_norm_biases: float32 [4, 512], replicated, may hold values from -3 to 3
- wide_norm_gains: float32 [3, 2048], replicated, may hold values from 0.5 to 1.5
- wide_norm_biases: float32 [3, 2048], replicated, may hold values from -3 to 3
- loss_slope_wrt_final: float32 [96, 8, 8, 2048], P('frames', 'rows'), may hold values from -6 to 6
Outputs:
- layer_output: float32 [96, 8, 8, 2048], P('frames', 'rows')
- grad_pixels: float32 [96, 16, 16, 1024], P('frames', 'rows')
- grad_narrower: float32 [1024, 512], P(None, 'rows')
- grad_strider: float32 [3, 3, 512, 512], P(None, None, None, 'rows')
- grad_widener: float32 [512, 2048], P(None, 'rows')
- grad_shortcut: float32 [1024, 2048], P(None, 'rows')
- grad_squeezer: float32 [2048, 512], P(None, 'rows')
- grad_condenser: float32 [512, 32], P(None, 'rows')
- grad_stencil: float32 [3, 3, 32, 32], P(None, None, None, 'rows')
- grad_exciter: float32 [32, 512], P(None, 'rows')
- grad_temporal: float32 [3, 384], P(None, 'rows')
- grad_kernels: float32 [3, 3, 3, 128, 128], P(None, None, None, None, 'rows')
- grad_restorer: float32 [512, 2048], P(None, 'rows')
- grad_scaling: float32 [4, 512], replicated
- grad_biasing: float32 [4, 512], replicated
- grad_amplitudes: float32 [3, 2048], replicated
- baseline_gradient: float32 [3, 2048], replicated
Inputs may be any that keep to these rules, and one draw needn't show every extreme that they name: `sequence_slot_lookup`: the offset of each frame within its clip. Clips are runs of 8 or 32 frames laid end to end from frame 0; each aligned run of 96 frames holds one clip of 32 frames and eight of 8. `sequence_span_lookup`: the length of the clip that holds each frame, consistent with sequence_slot_lookup.
All inputs are finite; a program needn't handle non-finite values.
Results may differ from a plain program's by a relative error of at most 0.0003.
Values sent between devices are 32-bit elements; how exact they have to be, the bound alone decides.
A program may use at most 192 MiB of HBM per device.

v0:
```python
import itertools
import math
from types import SimpleNamespace

import jax
import jax.numpy as jnp
from jax import lax
from jax.experimental import pallas as pl
from jax.experimental.pallas import tpu as pltpu
from jax.sharding import PartitionSpec as P

MESH = pl.DeviceIdType.MESH
EPSILON = 1e-05
VMEM_BYTES = 65400 * 2**10


def split(value):
    high = value.astype(jnp.bfloat16)
    return high, (value - high.astype(jnp.float32)).astype(jnp.bfloat16)


def put(pair_ref, index, value):
    high, low = split(value)
    pair_ref[(0,) + index] = high
    pair_ref[(1,) + index] = low


def product(stacked, weights, turned=False):
    result = lax.dot_general(
        stacked,
        weights,
        (((1,), (1 if turned else 0,)), ((), ())),
        preferred_element_type=jnp.float32,
    )
    half = result.shape[0] // 2
    return result[:half] + result[half:]


def small_product(value, weights, turned=False):
    return product(jnp.concatenate(split(value), 0), weights, turned)


def small_outer(left, right):
    def one(a, b):
        return lax.dot_general(
            a, b, (((0,), (0,)), ((), ())), preferred_element_type=jnp.float32
        )

    (a, b), (c, d) = split(left), split(right)
    return one(a, c) + one(a, d) + one(b, c)


def slope(value):
    logistic = jax.nn.sigmoid(value)
    return logistic * (1.0 + value * (1.0 - logistic))


def silu(value):
    return value * jax.nn.sigmoid(value)


def folded(value):
    return jnp.sum(value.reshape(-1, 8, value.shape[-1]), axis=0)


def moved_down(value):
    place = lax.broadcasted_iota(jnp.int32, value.shape, 0)
    return jnp.where(lax.rem(place, 8) == 0, 0.0, pltpu.roll(value, 1, 0))


def moved_up(value):
    place = lax.broadcasted_iota(jnp.int32, value.shape, 0)
    return jnp.where(lax.rem(place, 8) == 7, 0.0, pltpu.roll(value, value.shape[0] - 1, 0))


def chunks(total, step):
    def bind(body):
        @pl.loop(0, total // step)
        def _(place):
            body(pl.ds(pl.multiple_of(place * step, step), step))

    return bind


PUMPS = (1, 1, 1, 1, 1, 1, 1, 1, 1, 1, 1, 1)


def chain_kernel(names, dims, *refs):
    frames, rows, depth, a_count, b_count = dims
    m = SimpleNamespace(**dict(zip(names, refs)))
    f = lax.axis_index("frames")
    r = lax.axis_index("rows")
    after_f, before_f = lax.rem(f + 1, frames), lax.rem(f + frames - 1, frames)
    band = depth * 8
    half = 2 * band
    number_half = float(half * frames * rows)
    number_full = 4.0 * number_half
    above, below = r > 0, r < rows - 1
    above_one, below_one = jnp.where(above, 1.0, 0.0), jnp.where(below, 1.0, 0.0)
    wide = 2048

    loads = []

    def load(source, target, sem=None):
        if sem is None:
            sem = m.load_sem.at[len(loads)]
            loads.append(sem)
        copy = pltpu.make_async_copy(source, target, sem)
        copy.start()
        return copy

    def wait_row(row):
        block = m.xs.at[:, :, row]
        pltpu.make_async_copy(block, block, m.row_sem.at[row]).wait()

    lanes = [slice(k * 128, k * 128 + 128) for k in range(8)]

    def load_row(row):
        [
            load(m.x.at[:, row, :, lane], m.xs.at[k, :, row], m.row_sem.at[row])
            for k, lane in enumerate(lanes)
        ]

    for row in (3, 0, 1, 2):
        load_row(row)
    small_loads = [
        load(getattr(m, name + "_h"), getattr(m, name))
        for name in (
            "wer", "kst", "wex", "taps_in", "gain", "bias", "wide_gain", "wide_bias"
        )
    ]
    wn_load = load(m.wn_h, m.wn)
    wsk_load = load(m.wsk_h, m.wsk)
    ks_load = load(m.ks_h, m.ks)
    we_load = load(m.we_h, m.we)
    wcr_load = load(m.wcr_h, m.wcr)
    wce_load = load(m.wce_h, m.wce)
    kern_load = load(m.kern_h, m.kern)
    slope_loads = [load(m.slope_h.at[:, row], m.slope.at[row]) for row in range(2)]

    barrier = pltpu.get_barrier_semaphore()
    partners = [(f, lax.rem(r + step, rows)) for step in range(1, rows)]
    partners += [(lax.rem(f + step, frames), r) for step in range(1, frames)]
    for other in (after_f, before_f):
        partners += [(other, lax.rem(r + step, rows)) for step in range(1, rows)]
    if frames == 8:
        for chip_step in range(1, frames // 2):
            other = lax.rem(f + 2 * chip_step, frames)
            partners += [(other, lax.rem(r + step, rows)) for step in range(1, rows)]
    for partner in partners:
        pl.semaphore_signal(barrier, inc=1, device_id=partner, device_id_type=MESH)
    pl.semaphore_wait(barrier, len(partners))

    sent = []

    def send(source, target, send_sem, recv_sem, device):
        copy = pltpu.make_async_remote_copy(
            src_ref=source,
            dst_ref=target,
            send_sem=send_sem,
            recv_sem=recv_sem,
            device_id=device,
            device_id_type=MESH,
        )
        copy.start()
        return copy

    class Sum:
        count = 0

        def __init__(self, pieces):
            self.set = Sum.count % 2
            Sum.count += 1
            place = 0
            for piece in pieces:
                for k in range(piece.shape[1] // 128):
                    m.ar_in[self.set, place : place + 1, :] = piece[:, k * 128 : k * 128 + 128]
                    place += 1
            self.size = -(-place // 8) * 8
            half_f, core_f = f // 2, lax.rem(f, 2)
            self.first = (
                (m.ar_rows_a, m.ar_rows_b), m.ar_rs, m.ar_rr, r, rows, lambda other: (f, other)
            )
            self.second = (
                (m.ar_frames_a, m.ar_frames_b), m.ar_fs, m.ar_fr, f, frames, lambda other: (other, r)
            )
            if frames == 8 and self.size == 8:
                self.first = (
                    *self.first[:3], core_f, 2, lambda other: (f - core_f + other, r)
                )
                self.second = (
                    (m.ar_small.at[0], m.ar_small.at[1]), m.ar_fs, m.ar_fr,
                    half_f * rows + r, frames // 2 * rows,
                    lambda other: (other // rows * 2 + core_f, lax.rem(other, rows)),
                )
            self.copies = self.spread(m.ar_in, *self.first)

        def spread(self, source, slots, send_sem, recv_sem, me, count, device):
            piece = source.at[self.set, pl.ds(0, self.size)]
            copies = []
            for step in range(1, count):
                copies.append(
                    send(
                        piece,
                        slots[self.set].at[step, pl.ds(0, self.size)],
                        send_sem.at[self.set, step],
                        recv_sem.at[self.set, step],
                        device(lax.rem(me + step, count)),
                    )
                )
            return copies

        def gather(self, source, slots, send_sem, recv_sem, me, count, device):
            for copy in self.copies:
                copy.wait_recv()
            slots = slots[self.set]
            slots[0, : self.size] = source[self.set, : self.size]
            total = slots[me, : self.size]
            for other in range(1, count):
                spot = lax.rem(me + count - other, count)
                total = total + slots[spot, : self.size]
            return total

        def middle(self):
            first = self.copies
            m.ar_part[self.set, : self.size] = self.gather(m.ar_in, *self.first)
            self.copies = self.spread(m.ar_part, *self.second)
            for copy in first:
                copy.wait_send()

        def finish(self, *sizes):
            m.ar_out[: self.size] = self.gather(m.ar_part, *self.second)
            for copy in self.copies:
                copy.wait_send()
            results, place = [], 0
            for size in sizes:
                parts = []
                for k in range(size // 128):
                    parts.append(m.ar_out[place : place + 1, :])
                    place += 1
                results.append(jnp.concatenate(parts, axis=1))
            return results

        def all(self, *sizes):
            self.middle()
            return self.finish(*sizes)

    def settle(k, totals, squares, number, gain, bias):
        size = totals.shape[1]
        center = totals / number
        spread = lax.rsqrt(squares / number - center * center + EPSILON)
        scale = spread * gain
        m.vec[6 * k : 6 * k + 1, :size] = center
        m.vec[6 * k + 1 : 6 * k + 2, :size] = spread
        m.vec[6 * k + 2 : 6 * k + 3, :size] = scale
        m.vec[6 * k + 3 : 6 * k + 4, :size] = bias - center * scale

    def settle_back(k, bias_grad, gain_grad, number):
        size = bias_grad.shape[1]
        m.vec[6 * k + 4 : 6 * k + 5, :size] = bias_grad / number
        m.vec[6 * k + 5 : 6 * k + 6, :size] = gain_grad / number

    def vec(k, which, cols=slice(0, 512)):
        return m.vec[6 * k + which : 6 * k + which + 1, cols]

    def affine(k, value, cols=slice(0, 512)):
        return value * vec(k, 2, cols) + vec(k, 3, cols)

    def normed(k, value, cols=slice(0, 512)):
        return (value - vec(k, 0, cols)) * vec(k, 1, cols)

    def field_grad(k, grads, value, cols=slice(0, 512)):
        return vec(k, 2, cols) * (
            grads - vec(k, 4, cols) - normed(k, value, cols) * vec(k, 5, cols)
        )

    def clear():
        m.stat[...] = jnp.zeros_like(m.stat)

    def collect(k, value, cols=slice(0, 512)):
        m.stat[k, :, cols] = m.stat[k, :, cols] + folded(value)

    def collected(k, size=512):
        return jnp.sum(m.stat[k, :, :size], axis=0, keepdims=True)

    def column_tiles(body):
        @pl.loop(0, wide // 512)
        def _(place):
            body(pl.ds(pl.multiple_of(place * 512, 512), 512))

    c = lax.rem(f, 2)
    ib = lax.rem(f // 2, b_count)
    ia = f // (2 * b_count)
    flip1 = r + 1 - 2 * lax.rem(r, 2)
    flip2 = lax.rem(r + 2, rows)
    core = (f + 1 - 2 * c, r)
    thin = 512 // frames

    def a_peer(step):
        other = lax.rem(ia + step, a_count)
        return other, ((other * b_count + ib) * 2 + c, r)

    def b_peer(step):
        other = lax.rem(ib + step, b_count)
        return other, ((ia * b_count + other) * 2 + c, r)

    def add_blocks(target, source, lead=()):
        for index in itertools.product(*[range(size) for size in lead]):
            into, other = target.at[index], source.at[index]

            size = min(thin, 32 if into.shape[-1] > 128 else 64)

            @pl.loop(0, thin // size)
            def _(place):
                spot = pl.ds(pl.multiple_of(place * size, size), size)
                into[spot, :] = into[spot, :] + other[spot, :]

    def column_part(index):
        return pl.ds(pl.multiple_of(index * 128, 128), 128)

    ring = m.g_rows.shape[0]

    def unit_steps(fill, out, turn, kind):
        two, three, deep = turn % 2, turn % 3, turn % ring
        own, away, near = m.g_own.at[kind, two], m.g_away.at[kind], m.g_near.at[kind, two]
        bank = [m.g_send.at[kind, deep], m.g_recv.at[kind, deep]]
        used = [0]

        def go(source, target, device):
            spot = used[0]
            used[0] += 1
            return send(source, target, bank[0].at[spot], bank[1].at[spot], device)

        def done(copies):
            for copy in copies:
                copy.wait_recv()
            for copy in copies:
                copy.wait_send()

        def over_axis(count, peer, pick, buffer, lead):
            copies = []
            for step in range(1, count):
                other, device = peer(step)
                copies.append(go(pick(other), buffer.at[step - 1], device))
            yield
            done(copies)
            for step in range(2, count):
                add_blocks(buffer.at[0], buffer.at[step - 1], lead)

        def over_a(pick, buffer, lead):
            yield from over_axis(a_count, a_peer, pick, buffer, lead)
            add_blocks(buffer.at[0], pick(ia), lead)

        def over_b(pick, buffer, lead):
            yield from over_axis(b_count, b_peer, pick, buffer, lead)
            add_blocks(buffer.at[0], pick(ib), lead)

        def over_rows(pick, buffer, last, lead):
            copies = [go(pick(lax.rem(flip1, 2) + 2 * k), buffer.at[k], (f, flip1)) for k in range(2)]
            yield
            done(copies)
            for k in range(2):
                add_blocks(buffer.at[k], pick(lax.rem(r, 2) + 2 * k), lead)
            copies = [go(buffer.at[1 - r // 2], last, (f, flip2))]
            yield
            done(copies)
            add_blocks(last, buffer.at[r // 2], lead)

        fill(away, 1 - c)
        copies = [go(away, near, core)]
        fill(own, c)
        yield
        done(copies)
        add_blocks(own, near, (a_count, b_count))
        if kind == 0:
            first, second = m.g_first_p.at[deep], m.g_second_p.at[three]
            yield from over_b(lambda i: own.at[:, i], first, (a_count,))
            yield from over_a(lambda i: first.at[0, i], second, ())
        if kind == 1:
            first, second = m.g_first_q.at[deep], m.g_second_q.at[three]
            yield from over_a(lambda i: own.at[i], first, (b_count,))
            yield from over_b(lambda i: first.at[0, i], second, ())
        if kind < 2:
            final = m.g_fourth.at[kind, three]
            yield from over_rows(
                lambda i: second.at[0, :, column_part(i)], m.g_third.at[kind, three], final, ()
            )
        else:
            both = m.g_both.at[three]
            yield from over_rows(
                lambda i: own.at[:, :, :, column_part(i)],
                m.g_rows.at[deep],
                both,
                (a_count, b_count),
            )
            first, second = m.g_first_z.at[three], m.g_second_z.at[three]
            yield from over_a(lambda i: both.at[i], first, (b_count,))
            yield from over_b(lambda i: first.at[0, i], second, ())
            final = second.at[0]
        orders = ((b_count, b_peer), (a_count, a_peer))
        (one_count, one_peer), (two_count, two_peer) = orders[:: 1 if kind % 2 == 0 else -1]
        local = pltpu.make_async_copy(final, out.at[c, ia, ib], bank[1].at[used[0]])
        used[0] += 1
        local.start()
        copies = []
        for step in range(1, one_count):
            _, device = one_peer(step)
            copies.append(go(final, out.at[c, ia, ib], device))
        yield
        local.wait()
        done(copies)
        copies = []
        field = out.at[c, ia] if kind % 2 == 0 else out.at[c, :, ib]
        for step in range(1, two_count):
            _, device = two_peer(step)
            copies.append(go(field, field, device))
        yield
        done(copies)
        copies = [go(out.at[c], out.at[c], core)]
        yield
        done(copies)

    units, active, begun = [], [], [0]

    def advance():
        kept = []
        for age, group in active:
            group = [unit for unit in group if next(unit, active) is not active]
            if group:
                kept.append((age + 1, group))
        active[:] = kept
        if units:
            group = []
            for kind in range(3):
                if units:
                    fill, out = units.pop(0)
                    group.append(unit_steps(fill, out, begun[0], kind))
            begun[0] += 1
            for unit in group:
                next(unit)
            active.append((1, group))

    def pump(count):
        if count is None:
            while units or active:
                advance()
        else:
            for _ in range(count):
                advance()

    def begin_all_but(count):
        while len(units) > count:
            advance()

    def outer(left, right):
        def one(a, b):
            return lax.dot_general(
                a, b, (((0,), (0,)), ((), ())), preferred_element_type=jnp.float32
            )

        (high, low), (grad_high, grad_low) = left, right
        both = one(high, jnp.concatenate([grad_high, grad_low], 1))
        size = grad_high.shape[1]
        return both[:, :size] + both[:, size:] + one(low, grad_high)

    def blocks(value):
        return value.reshape(a_count, b_count, thin, value.shape[-1])

    def filler(left, right):
        def fill(target, which):
            start = pl.multiple_of(which * 256, 256)
            target[...] = blocks(
                outer([left(k, start) for k in range(2)], [right(k) for k in range(2)])
            )

        return fill

    def lanes_of(ref, quarter):
        def pick(k):
            return jnp.concatenate(
                [ref[k, :, z * 512 + quarter * 128 : z * 512 + quarter * 128 + 128] for z in range(4)],
                1,
            )

        return pick

    def whole(ref):
        return lambda k: ref[k]

    def rows_from(ref, base):
        return lambda k, start: ref[k, :, pl.ds(base + start, 256)]

    def out_lanes(ref, quarter):
        return ref.at[:, :, :, :, pl.ds(quarter * 128, 128)]

    def add_restorer():
        for quarter in range(4):
            units.append(
                (
                    filler(rows_from(m.squashed, 0), lanes_of(m.gc2, quarter)),
                    out_lanes(m.restorer, quarter),
                )
            )

    def add_widener():
        for quarter in range(4):
            units.append(
                (
                    filler(rows_from(m.h2, 0), lanes_of(m.uh, quarter)),
                    out_lanes(m.widener, quarter),
                )
            )

    def add_shortcut():
        def sampled(base):
            def pick(k, start):
                lane = pl.ds(base + start, 256)
                return jnp.concatenate(
                    [m.xb[k, pl.ds(row * half, band), lane] for row in (0, 2)], 0
                )

            return pick

        for quarter in range(4):
            for place in range(2):
                units.append(
                    (
                        filler(sampled(place * 512), lanes_of(m.gc2, quarter)),
                        out_lanes(m.shortcut.at[place], quarter),
                    )
                )

    def add_squeezer():
        for place in range(4):
            units.append(
                (filler(rows_from(m.uh, place * 512), whole(m.ga2)), m.squeezer.at[place])
            )

    def add_strider():
        def tapped(dy, base):
            def pick(k, start):
                lane = pl.ds(base + start, 256)
                return jnp.concatenate([m.pc[k, dy + 2 * i, :, lane] for i in range(2)], 0)

            return pick

        def grads(k):
            return jnp.concatenate([m.gb[k, i, :, 0:512] for i in range(2)], 0)

        for dy in range(3):
            for dx in range(3):
                units.append((filler(tapped(dy, dx * 512), grads), m.strider.at[dy * 3 + dx]))

    def add_narrower():
        def grads(k):
            return jnp.concatenate([m.uh[k, :, i * 512 : i * 512 + 512] for i in range(4)], 0)

        for place in range(2):
            units.append(
                (filler(rows_from(m.xb, place * 512), grads), m.narrower.at[place])
            )

    def one_hot(shape, places):
        row = lax.broadcasted_iota(jnp.int32, shape, 0)
        lane = lax.broadcasted_iota(jnp.int32, shape, 1)
        return jnp.where(row == places(lane), 1.0, 0.0).astype(jnp.bfloat16)

    def add_pack():
        def put_rows(start, z, value):
            spot = start % 64 // 16
            m.xs[z * 2 + start // 512, start % 512 // 64, spot : spot + 2] = value.reshape(2, 16, 128)

        for k in range(3):
            left = [m.gk[p, k] for p in range(2)]
            for dy in range(3):
                right = [
                    jnp.concatenate([m.mixed[p, k, i + dy] for i in range(2)], 0) for p in range(2)
                ]
                value = outer(left, right)
                for dx in range(3):
                    for z in range(4):
                        put_rows(
                            ((k * 3 + dy) * 3 + dx) * 32,
                            z,
                            value[z * 32 : z * 32 + 32, dx * 128 : dx * 128 + 128],
                        )

        def tap_places(lane):
            inside = lax.rem(lane, 128)
            return jnp.where(inside < 96, lax.div(lane, 128) * 96 + inside, -1)

        temporal = small_product(
            jnp.concatenate([m.temporal[...], jnp.zeros((5, 384), jnp.float32)], 0),
            one_hot((384, 512), tap_places),
        )
        for z in range(4):
            own_lanes = slice(z * 128, z * 128 + 128)
            eight = slice(z * 8, z * 8 + 8)
            put_rows(
                864,
                z,
                jnp.concatenate(
                    [m.condenser[eight, q * 128 : q * 128 + 128] for q in range(4)], 0
                ),
            )
            put_rows(
                896,
                z,
                jnp.concatenate(
                    [m.stencil[eight, q * 128 : q * 128 + 128] for q in range(3)]
                    + [temporal[:, own_lanes]],
                    0,
                ),
            )
            put_rows(928, z, m.exciter[:, own_lanes])

        for place in range(2):

            def fill(target, which, place=place):
                for lt in range(4):
                    value = m.xs[lt * 2 + place, pl.ds(which * 4, 4)]
                    target[:, :, :, lt * 128 : lt * 128 + 128] = blocks(value.reshape(256, 128))

            units.append((fill, m.pack.at[place]))


    for frame in range(depth):
        for mask, tall, flat_mask in (
            (m.place_of[frame] > 0, m.before_band, m.before16),
            (m.place_of[frame] < m.length_of[frame] - 1, m.after_band, m.after16),
        ):
            one = jnp.where(mask, 1.0, 0.0)
            tall[frame * 8 : frame * 8 + 8, :] = jnp.full((8, 128), one)
            flat_mask[frame : frame + 1, :] = jnp.full((1, 128), one)
    for flat_mask in (m.before16, m.after16):
        flat_mask[depth:, :] = jnp.zeros((flat_mask.shape[0] - depth, 128), jnp.float32)
    clear()

    @pl.when(r == 0)
    def _():
        m.a[0] = jnp.zeros(m.a.shape[1:], jnp.float32)

    @pl.when(r == rows - 1)
    def _():
        m.b_halo[...] = jnp.zeros_like(m.b_halo)
        m.back_halo[...] = jnp.zeros_like(m.back_halo)

    for buffers in (m.source, m.grad_pad):
        for k in range(buffers.shape[0]):

            @pl.when(r == 0)
            def _():
                buffers[k, 0] = jnp.zeros(buffers.shape[2:], jnp.float32)

            @pl.when(r == rows - 1)
            def _():
                buffers[k, 3] = jnp.zeros(buffers.shape[2:], jnp.float32)

    def reduce_row(row):
        @pl.loop(0, depth // 2)
        def _(pair):
            for parity in range(2):
                spot = pl.ds(parity, 8, stride=2)
                place = pl.multiple_of(row * half + parity * band + pair * 16, 16)
                for k, lane in enumerate(lanes):
                    value = jnp.concatenate(
                        [m.xs[k, 2 * pair, row, spot, :], m.xs[k, 2 * pair + 1, row, spot, :]], 0
                    )
                    put(m.xb, (pl.ds(place, 16), lane), value)

        place = pl.ds(pl.multiple_of(row * half, half), half)
        result = product(jnp.concatenate([m.xb[0, place, :], m.xb[1, place, :]], 0), m.wn[...])
        m.a[1 + row] = result.reshape(2, band, 512)
        collect(0, result)
        collect(1, result * result)

    wait_row(3)
    wn_load.wait()
    reduce_row(3)

    @pl.when(below)
    def _():
        send(m.a.at[4], m.a.at[0], m.halo_s.at[0], m.halo_r.at[0], (f, r + 1))

    for row in range(3):
        wait_row(row)

    @pl.loop(0, 3)
    def _(row):
        reduce_row(row)

    total = Sum([collected(0), collected(1)])
    clear()
    wsk_load.wait()

    def shortcut_tile(cols):
        lhs = jnp.concatenate(
            [m.xb[k, pl.ds(row * half, band), :] for k in range(2) for row in (0, 2)], 0
        )
        result = product(lhs, m.wsk[:, cols])
        m.s[:, cols] = result
        collect(2, result, cols)
        collect(3, result * result, cols)

    @pl.loop(0, 2)
    def _(place):
        shortcut_tile(pl.ds(pl.multiple_of(place * 512, 512), 512))

    total.middle()

    @pl.loop(2, 4)
    def _(place):
        shortcut_tile(pl.ds(pl.multiple_of(place * 512, 512), 512))

    totals, squares = total.finish(512, 512)
    for copy in small_loads:
        copy.wait()
    m.taps[...] = m.taps_in[...].astype(jnp.float32)
    settle(0, totals, squares, number_full, m.gain[0:1], m.bias[0:1])

    def activate(row, keep):
        @chunks(band, 32)
        def _(spot):
            for parity in range(2):
                value = silu(affine(0, m.a[row, parity, spot, :]))
                if keep is not None:
                    value = value * keep
                if parity == 0:
                    put(m.pc, (row, spot, slice(512, 1024)), value)
                else:
                    put(m.pc, (row, spot, slice(1024, 1536)), value)
                    put(m.pc, (row, spot, slice(0, 512)), moved_down(value))

    @pl.loop(1, 5)
    def _(row):
        activate(row, None)

    @pl.when(above)
    def _():
        pltpu.make_async_remote_copy(
            src_ref=m.a.at[4],
            dst_ref=m.a.at[0],
            send_sem=m.halo_s.at[0],
            recv_sem=m.halo_r.at[0],
            device_id=(f, lax.rem(r + 1, rows)),
            device_id_type=MESH,
        ).wait_recv()

    activate(0, above_one)
    ks_load.wait()

    def strided(dy):
        return product(
            jnp.concatenate([m.pc[k, dy + 2 * i] for k in range(2) for i in range(2)], 0), m.ks[dy]
        )

    m.b[...] = strided(0)
    m.b[...] = m.b[...] + strided(1)
    result = m.b[...] + strided(2)
    m.b[...] = result
    collect(0, result)
    collect(1, result * result)

    @pl.when(above)
    def _():
        send(
            m.b.at[pl.ds(0, band)], m.b_halo, m.halo_s.at[1], m.halo_r.at[1], (f, r - 1)
        )

    totals, squares, totals_p, squares_p = Sum(
        [collected(0), collected(1), collected(2, wide), collected(3, wide)]
    ).all(512, 512, wide, wide)
    clear()
    settle(1, totals, squares, number_half, m.gain[1:2], m.bias[1:2])
    settle(5, totals_p, squares_p, number_half, m.wide_gain[1:2], m.wide_bias[1:2])

    @chunks(half, 32)
    def _(spot):
        put(m.h2, (spot, slice(None)), silu(affine(1, m.b[spot, :])))

    we_load.wait()

    @column_tiles
    def _(cols):
        result = product(jnp.concatenate([m.h2[0], m.h2[1]], 0), m.we[:, cols])
        m.c[:, cols] = result
        collect(0, result, cols)
        collect(1, result * result, cols)

    totals, squares = Sum([collected(0, wide), collected(1, wide)]).all(wide, wide)
    clear()
    settle(4, totals, squares, number_half, m.wide_gain[0:1], m.wide_bias[0:1])

    def first_sum(spot, cols):
        return affine(4, m.c[spot, cols], cols) + affine(5, m.s[spot, cols], cols)

    @column_tiles
    def _(cols):
        @chunks(half, 32)
        def _(spot):
            value = silu(first_sum(spot, cols))
            put(m.uh, (spot, cols), value)

    wcr_load.wait()
    result = product(jnp.concatenate([m.uh[0], m.uh[1]], 0), m.wcr[...])
    m.d[...] = result
    collect(0, result)
    collect(1, result * result)
    totals, squares = Sum([collected(0), collected(1)]).all(512, 512)
    clear()
    settle(2, totals, squares, number_half, m.gain[2:3], m.bias[2:3])

    @chunks(half, 32)
    def _(spot):
        m.hid[spot, :] = silu(affine(2, m.d[spot, :]))

    m.edge[...] = jnp.zeros_like(m.edge)
    for row in range(2):
        block = m.hid[row * band : row * band + band, :]
        column = lax.rem(lax.broadcasted_iota(jnp.int32, block.shape, 0), 8)
        for k, value in enumerate(
            (block, jnp.where(column == 0, block, 0.0), jnp.where(column == 7, block, 0.0))
        ):
            m.edge[k, row, :depth] = jnp.sum(value.reshape(depth, 8, 512), axis=1)
    pad = m.edge.shape[2]
    reduced = small_product(m.edge[...].reshape(6 * pad, 512), m.wer[...], True)

    def part(kind, row):
        start = (kind * 2 + row) * pad
        return reduced[start : start + pad]

    taps = []
    for dy in range(3):
        for dx in range(3):
            by_row = []
            for row in range(2):
                value = part(0, row)
                if dx == 0:
                    value = value - part(2, row)
                if dx == 2:
                    value = value - part(1, row)
                by_row.append(value)
            if dy == 0:
                by_row[1] = by_row[1] * below_one
            if dy == 2:
                by_row[0] = by_row[0] * above_one
            taps.append(by_row[0] + by_row[1])
    taps.append(jnp.zeros((pad, 96), jnp.float32))
    m.tap_in[...] = jnp.concatenate(taps, 1)

    def rows_sum(source, slots, near, near_slots, toward, sems):
        copies = []
        for step in range(1, rows):
            copies.append(
                send(
                    source,
                    slots.at[step],
                    m.rows_s.at[sems, step],
                    m.rows_r.at[sems, step],
                    (f, lax.rem(r + step, rows)),
                )
            )
        for step in range(rows):
            copies.append(
                send(
                    source.at[near],
                    near_slots.at[step],
                    m.rows_s.at[sems, rows + step],
                    m.rows_r.at[sems, rows + step],
                    (toward, lax.rem(r + step, rows)),
                )
            )
        slots[0] = source[...]
        for copy in copies:
            copy.wait_recv()
        total = slots[r]
        other_total = near_slots[r]
        for other in range(1, rows):
            spot = lax.rem(r + rows - other, rows)
            total = total + slots[spot]
            other_total = other_total + near_slots[spot]
        for copy in copies:
            copy.wait_send()
        return total, other_total

    current, later = rows_sum(
        m.tap_in, m.tap_slots, pl.ds(0, 8), m.tap_near, before_f, 0
    )
    place = lax.broadcasted_iota(jnp.int32, current.shape, 0)
    follow = pltpu.roll(current, pad - 1, 0)
    follow = jnp.where(place == depth - 1, later[0:1], follow)
    after16 = m.after16[...]
    before16 = m.before16[...]
    follow = jnp.where(place < depth, follow, 0.0) * jnp.concatenate([after16] * 3, 1)
    m.follow[...] = follow
    area = float(16 * rows)
    pooled = (
        (small_product(follow[:, :288], m.kst[...]) - current[:, 128:160])
        * after16[:, :32]
        / area
    )
    m.pooled[...] = pooled
    m.gate[...] = jax.nn.sigmoid(small_product(pooled, m.wex[...]))
    for frame in range(depth):
        m.gate_all[frame * 8 : frame * 8 + 8, :] = jnp.broadcast_to(
            1.0 + m.gate[frame : frame + 1, :], (8, 512)
        )

    def halo(field, sems, pumps=0):
        own, first, last = pl.ds(8, band), pl.ds(8, 8), pl.ds(band, 8)
        low, high = pl.ds(0, 8), pl.ds(band + 8, 8)
        moves = [
            (field.at[pl.ds(1, 2), last], field.at[pl.ds(1, 2), low], (after_f, r), None, None),
            (field.at[pl.ds(1, 2), first], field.at[pl.ds(1, 2), high], (before_f, r), None, None),
            (field.at[2, own], field.at[0, own], (f, r + 1), below, above),
            (field.at[1, own], field.at[3, own], (f, r - 1), above, below),
            (field.at[2, last], field.at[0, low], (after_f, r + 1), below, above),
            (field.at[1, last], field.at[3, low], (after_f, r - 1), above, below),
            (field.at[2, first], field.at[0, high], (before_f, r + 1), below, above),
            (field.at[1, first], field.at[3, high], (before_f, r - 1), above, below),
        ]
        copies = []
        for k, (source, target, device, able, arriving) in enumerate(moves):
            copies.append(
                pltpu.make_async_remote_copy(
                    src_ref=source,
                    dst_ref=target,
                    send_sem=m.ring_s.at[sems % 2, k],
                    recv_sem=m.ring_r.at[sems % 2, k],
                    device_id=device,
                    device_id_type=MESH,
                )
            )
        for copy, move in zip(copies, moves):
            if move[3] is None:
                copy.start()
            else:
                pl.when(move[3])(copy.start)
        pump(pumps)
        for copy, move in zip(copies, moves):
            if move[4] is None:
                copy.wait_recv()
            else:
                pl.when(move[4])(copy.wait_recv)
        for copy, move in zip(copies, moves):
            if move[3] is None:
                copy.wait_send()
            else:
                pl.when(move[3])(copy.wait_send)

    own = pl.ds(8, band)
    previous, following = pl.ds(0, band), pl.ds(16, band)
    before_band = m.before_band[...]
    after_band = m.after_band[...]

    def sides(value):
        return jnp.concatenate([moved_down(value), value, moved_up(value)], 1)

    m.merged[:, 0:128] = jnp.concatenate(
        [m.hid[i * band : i * band + band, 0:128] * m.gate_all[:, 0:128] for i in range(2)], 0
    )
    kern_load.wait()
    for k in range(3):
        cols = slice((k + 1) * 128, (k + 2) * 128)
        for i in range(2):
            rows_i = slice(i * band, i * band + band)
            value = m.hid[rows_i, cols] * m.gate_all[:, cols]
            if k > 0:
                value = value + m.merged[rows_i, k * 128 : (k + 1) * 128]
            m.source[k, 1 + i, own] = value
        halo(m.source.at[k], k)
        tap = [m.taps[i : i + 1, k * 128 : (k + 1) * 128] for i in range(3)]
        for i in range(4):
            mixed = (
                tap[0] * before_band * m.source[k, i, previous]
                + tap[1] * m.source[k, i, own]
                + tap[2] * after_band * m.source[k, i, following]
            )
            put(m.mixed, (k, i), sides(mixed))
        result = jnp.zeros((half, 128), jnp.float32)
        for dy in range(3):
            lhs = jnp.concatenate([m.mixed[p, k, i + dy] for p in range(2) for i in range(2)], 0)
            result = result + product(lhs, m.kern[k, dy])
        m.merged[:, cols] = result

    result = m.merged[...]
    collect(0, result)
    collect(1, result * result)
    totals, squares = Sum([collected(0), collected(1)]).all(512, 512)
    clear()
    settle(3, totals, squares, number_half, m.gain[3:4], m.bias[3:4])

    @chunks(half, 32)
    def _(spot):
        put(m.squashed, (spot, slice(None)), silu(affine(3, m.merged[spot, :])))

    wce_load.wait()

    @column_tiles
    def _(cols):
        result = product(jnp.concatenate([m.squashed[0], m.squashed[1]], 0), m.wce[:, cols])
        m.e[:, cols] = result
        collect(0, result, cols)
        collect(1, result * result, cols)

    totals, squares = Sum([collected(0, wide), collected(1, wide)]).all(wide, wide)
    clear()
    settle(6, totals, squares, number_half, m.wide_gain[2:3], m.wide_bias[2:3])

    for copy in slope_loads:
        copy.wait()

    @column_tiles
    def _(cols):
        for row in range(2):

            @pl.loop(0, depth // 4)
            def _(part_place):
                block = pl.ds(pl.multiple_of(part_place * 4, 4), 4)
                spot = pl.ds(pl.multiple_of(row * band + part_place * 32, 32), 32)
                raw = m.e[spot, cols]
                value = (
                    affine(6, raw, cols)
                    + m.uh[0, spot, cols].astype(jnp.float32)
                    + m.uh[1, spot, cols].astype(jnp.float32)
                )
                logistic = jax.nn.sigmoid(value)
                grads = m.slope[row, block, :, cols].reshape(32, 512) * (
                    logistic * (1.0 + value * (1.0 - logistic))
                )
                m.slope[row, block, :, cols] = (value * logistic).reshape(4, 8, 512)
                m.d2[spot, cols] = grads
                collect(0, grads, cols)
                collect(1, grads * normed(6, raw, cols), cols)

    stores = []

    def store(source, target, sem=None):
        copy = pltpu.make_async_copy(source, target, m.store_sem.at[len(stores)] if sem is None else sem)
        copy.start()
        if sem is None:
            stores.append(copy)

    for row in range(2):
        store(m.slope.at[row], m.layer_output.at[:, row])

    bias_grad, gain_grad = Sum([collected(0, wide), collected(1, wide)]).all(wide, wide)
    clear()
    settle_back(6, bias_grad, gain_grad, number_half)
    m.baselines[2:3] = bias_grad
    m.amplitudes[2:3] = gain_grad

    @column_tiles
    def _(cols):
        @chunks(half, 32)
        def _(spot):
            put(m.gc2, (spot, cols), field_grad(6, m.d2[spot, cols], m.e[spot, cols], cols))


    def back_through(pair, weights, raw, k):
        m.back[...] = product(jnp.concatenate([pair[0], pair[1]], 0), weights[...], True)

        @chunks(half, 32)
        def _(spot):
            value = raw[spot, :]
            grads = m.back[spot, :] * slope(affine(k, value))
            m.back[spot, :] = grads
            collect(0, grads)
            collect(1, grads * normed(k, value))

    back_through(m.gc2, m.wce, m.merged, 3)
    add_restorer()
    total = Sum([collected(0), collected(1)])
    pump(PUMPS[0])
    bias_grad, gain_grad = total.all(512, 512)
    clear()
    settle_back(3, bias_grad, gain_grad, number_half)
    m.biasing[3:4] = bias_grad
    m.scaling[3:4] = gain_grad
    merged_grad = field_grad(3, m.back[...], m.merged[...])
    m.eg[...] = merged_grad

    for k in (2, 1, 0):
        cols = slice((k + 1) * 128, (k + 2) * 128)
        grads = m.eg[:, cols]
        if k < 2:
            grads = grads + m.eg[:, (k + 2) * 128 : (k + 3) * 128]
        put(m.gk, (k,), grads)
        for i in range(2):
            m.grad_pad[k % 2, 1 + i, own] = grads[i * band : i * band + band]
        halo(m.grad_pad.at[k % 2], 3 + k, PUMPS[1 + k])
        for i in range(4):
            put(m.grad_sides, (i,), sides(m.grad_pad[k % 2, i]))
        result = jnp.zeros((2 * (band + 16), 128), jnp.float32)
        for dy in range(3):
            lhs = jnp.concatenate([m.grad_sides[p, i + dy] for p in range(2) for i in range(2)], 0)
            for dx in range(3):
                result = result + product(
                    lhs[:, dx * 128 : dx * 128 + 128],
                    m.kern[k, 2 - dy, (2 - dx) * 128 : (3 - dx) * 128, :],
                    True,
                )
        span = band + 16
        tap = [m.taps[i : i + 1, k * 128 : (k + 1) * 128] for i in range(3)]
        tap_grads = [0.0, 0.0, 0.0]
        for i in range(2):
            m.mixed_grad[i] = result[i * span : i * span + span]
            middle = m.mixed_grad[i, own]
            for j, value in enumerate(
                (
                    middle * before_band * m.source[k, 1 + i, previous],
                    middle * m.source[k, 1 + i, own],
                    middle * after_band * m.source[k, 1 + i, following],
                )
            ):
                tap_grads[j] = tap_grads[j] + jnp.sum(value, axis=0, keepdims=True)
            m.eg[i * band : i * band + band, cols] = (
                tap[2] * before_band * m.mixed_grad[i, previous]
                + tap[1] * middle
                + tap[0] * after_band * m.mixed_grad[i, following]
            )
        for j in range(3):
            m.temporal[j : j + 1, k * 128 : (k + 1) * 128] = tap_grads[j]


    gate = m.gate[...]
    m.gate_part[...] = jnp.zeros_like(m.gate_part)
    touched = m.eg[...] * m.hid[...]
    touched = jnp.sum(touched.reshape(2 * depth, 8, 512), axis=1)
    m.gate_part[:depth] = touched[:depth] + touched[depth:]
    m.gate_part[...] = m.gate_part[...] * gate * (1.0 - gate)
    current, earlier = rows_sum(
        m.gate_part, m.gate_slots, pl.ds(pad - 8, 8), m.gate_near, after_f, 1
    )
    place = lax.broadcasted_iota(jnp.int32, current.shape, 0)
    last_row = depth - 1 - (pad - 8)
    shifted = jnp.where(place == 0, earlier[last_row : last_row + 1], pltpu.roll(current, 1, 0))
    pooled_grads = small_product(jnp.concatenate([current, shifted], 0), m.wex[...], True) / area
    motion = pooled_grads[:pad] * after16[:, :32]
    motion_before = pooled_grads[pad:] * before16[:, :32]
    spread = small_product(motion_before, m.kst[...], True)

    def tap_value(dy, dx):
        start = (dy * 3 + dx) * 32
        return spread[:, start : start + 32]

    values = []
    by_row = []
    for row in range(2):
        columns = []
        for dx in range(3):
            if row == 0:
                value = tap_value(0, dx) + tap_value(1, dx)
                value = value + tap_value(2, dx) * above_one
            else:
                value = tap_value(1, dx) + tap_value(2, dx)
                value = value + tap_value(0, dx) * below_one
            columns.append(value)
        by_row.append(columns)
    for kind in range(3):
        for row in range(2):
            d0, d1, d2 = by_row[row]
            value = (d0 + d1 + d2, d0 + d1, d1 + d2)[kind]
            values.append(value - motion)
    reduced_grad = jnp.concatenate(values, 0)
    m.e[: 6 * pad, :512] = small_product(reduced_grad, m.wer[...])

    for row in range(2):

        @pl.loop(0, depth)
        def _(frame):
            spot = pl.ds(pl.multiple_of(row * band + frame * 8, 8), 8)

            def edge_line(kind):
                return m.e[pl.ds((kind * 2 + row) * pad + frame, 1), 0:512]

            column = lax.broadcasted_iota(jnp.int32, (8, 512), 0)
            extra = jnp.where(
                column == 0,
                edge_line(1),
                jnp.where(column == 7, edge_line(2), edge_line(0)),
            )
            raw = m.d[spot, :]
            grads = m.eg[spot, :] * m.gate_all[pl.ds(pl.multiple_of(frame * 8, 8), 8), :] + extra
            grads = grads * slope(affine(2, raw))
            m.back[spot, :] = grads
            collect(0, grads)
            collect(1, grads * normed(2, raw))

    total = Sum([collected(0), collected(1)])
    m.exciter[...] = small_outer(m.pooled[...], m.gate_part[...])
    m.stencil[...] = small_outer(motion, m.follow[...]) * (1.0 / rows)
    edges = jnp.concatenate([m.edge[0] - m.edge[1] - m.edge[2], m.edge[1], m.edge[2]], 0)
    m.condenser[...] = small_outer(reduced_grad, edges.reshape(6 * pad, 512))
    add_pack()
    pump(PUMPS[4])
    bias_grad, gain_grad = total.all(512, 512)
    clear()
    settle_back(2, bias_grad, gain_grad, number_half)
    m.biasing[2:3] = bias_grad
    m.scaling[2:3] = gain_grad

    @chunks(half, 32)
    def _(spot):
        put(m.ga2, (spot, slice(None)), field_grad(2, m.back[spot, :], m.d[spot, :]))


    @column_tiles
    def _(cols):
        m.e[:, cols] = product(jnp.concatenate([m.ga2[0], m.ga2[1]], 0), m.wcr[cols, :], True)

        @chunks(half, 32)
        def _(spot):
            grads = (m.d2[spot, cols] + m.e[spot, cols]) * slope(first_sum(spot, cols))
            m.d2[spot, cols] = grads
            collect(0, grads, cols)
            collect(1, grads * normed(4, m.c[spot, cols], cols), cols)
            collect(2, grads * normed(5, m.s[spot, cols], cols), cols)

    add_squeezer()
    total = Sum([collected(0, wide), collected(1, wide), collected(2, wide)])
    pump(PUMPS[5])
    total.middle()
    pump(PUMPS[6])
    bias_grad, gain_c, gain_p = total.finish(wide, wide, wide)
    clear()
    settle_back(4, bias_grad, gain_c, number_half)
    settle_back(5, bias_grad, gain_p, number_half)
    for k in range(2):
        m.baselines[k : k + 1] = bias_grad
    m.amplitudes[0:1] = gain_c
    m.amplitudes[1:2] = gain_p

    begin_all_but(0)

    @column_tiles
    def _(cols):
        @chunks(half, 32)
        def _(spot):
            grads = m.d2[spot, cols]
            put(m.uh, (spot, cols), field_grad(4, grads, m.c[spot, cols], cols))
            put(m.gc2, (spot, cols), field_grad(5, grads, m.s[spot, cols], cols))

    back_through(m.uh, m.we, m.b, 1)

    @pl.when(above)
    def _():
        send(
            m.back.at[pl.ds(0, band)], m.back_halo, m.halo_s.at[2], m.halo_r.at[2], (f, r - 1)
        )

    total = Sum([collected(0), collected(1)])
    clear()
    add_widener()
    add_shortcut()
    pump(PUMPS[7])

    for cols in (slice(0, 512), slice(512, 1024)):
        if cols.start:
            total.middle()
            pump(PUMPS[8])
        m.d2[:, cols] = product(jnp.concatenate([m.gc2[0], m.gc2[1]], 0), m.wsk[cols, :], True)

    bias_grad, gain_grad = total.finish(512, 512)
    settle_back(1, bias_grad, gain_grad, number_half)
    m.biasing[1:2] = bias_grad
    m.scaling[1:2] = gain_grad

    def strided_grad(row, spot, value):
        put(m.gb, (row, spot, slice(0, 512)), value)
        put(m.gb, (row, spot, slice(512, 1024)), moved_up(value))

    for row in range(2):

        @chunks(band, 32)
        def _(spot):
            place = pl.ds(pl.multiple_of(row * band + spot.start, 32), 32)
            strided_grad(row, spot, field_grad(1, m.back[place, :], m.b[place, :]))

    @pl.when(below)
    def _():
        for k, (source, target) in enumerate(((m.b, m.b_halo), (m.back, m.back_halo))):
            pltpu.make_async_remote_copy(
                src_ref=source.at[pl.ds(0, band)],
                dst_ref=target,
                send_sem=m.halo_s.at[1 + k],
                recv_sem=m.halo_r.at[1 + k],
                device_id=(f, lax.rem(r + 1, rows)),
                device_id_type=MESH,
            ).wait_recv()

    @chunks(band, 32)
    def _(spot):
        value = field_grad(1, m.back_halo[spot, :], m.b_halo[spot, :])
        strided_grad(2, spot, value * below_one)


    add_strider()
    pump(PUMPS[9])

    def gb_rows(first, variant):
        lanes = slice(variant * 512, variant * 512 + 512)
        return jnp.concatenate([m.gb[k, first + i, :, lanes] for k in range(2) for i in range(2)], 0)

    def tap_weights(dy, dx):
        return m.ks[dy, dx * 512 : dx * 512 + 512, :]

    @pl.when(above)
    def _():
        for k, source in enumerate((m.b, m.back)):
            pltpu.make_async_remote_copy(
                src_ref=source.at[pl.ds(0, band)],
                dst_ref=m.back_halo,
                send_sem=m.halo_s.at[1 + k],
                recv_sem=m.halo_r.at[1 + k],
                device_id=(f, lax.rem(r + 1, rows)),
                device_id_type=MESH,
            ).wait_send()

    def ha_rows(parity, spot):
        return pl.ds(pl.multiple_of(parity * band + spot.start, 32), 32)

    plan = {
        (0, 0): [(0, 0, 1, 1)],
        (1, 0): [(0, 0, 1, 2), (0, 1, 1, 0)],
        (0, 1): [(0, 0, 2, 1), (1, 0, 0, 1)],
        (1, 1): [(0, 0, 2, 2), (1, 0, 0, 2), (0, 1, 2, 0), (1, 1, 0, 0)],
    }
    for (parity, odd), terms in plan.items():
        result = None
        for first, variant, dy, dx in terms:
            value = product(gb_rows(first, variant), tap_weights(dy, dx), True)
            result = value if result is None else result + value
        m.back[...] = result
        for i in range(2):
            row = 2 * i + odd

            @chunks(band, 32)
            def _(spot):
                place = pl.ds(pl.multiple_of(i * band + spot.start, 32), 32)
                raw = m.a[1 + row, parity, spot, :]
                grads = m.back[place, :] * slope(affine(0, raw))
                m.e[ha_rows(parity, spot), row * 512 : row * 512 + 512] = grads
                collect(0, grads)
                collect(1, grads * normed(0, raw))

    total = Sum([collected(0), collected(1)])
    pump(PUMPS[10])
    total.middle()
    pump(PUMPS[11])
    bias_grad, gain_grad = total.finish(512, 512)
    settle_back(0, bias_grad, gain_grad, number_full)
    begin_all_but(17)
    m.biasing[0:1] = bias_grad
    m.scaling[0:1] = gain_grad

    @pl.loop(0, 4)
    def _(row):
        for parity in range(2):

            @chunks(band, 32)
            def _(spot):
                lane = pl.ds(pl.multiple_of(row * 512, 512), 512)
                value = field_grad(
                    0, m.e[ha_rows(parity, spot), lane], m.a[1 + row, parity, spot, :]
                )
                put(m.uh, (ha_rows(parity, spot), lane), value)

    add_narrower()
    pump(1)

    def pixel_row(row):
        lane = pl.ds(pl.multiple_of(row * 512, 512), 512)
        lhs = jnp.concatenate([m.uh[0, :, lane], m.uh[1, :, lane]], 0)
        for part_cols in (slice(0, 512), slice(512, 1024)):
            result = product(lhs, m.wn[part_cols, :], True)
            even = jnp.where(lax.rem(row, 2) == 0, 1.0, 0.0)
            shortcut = m.d2[pl.ds(pl.multiple_of((row // 2) * band, band), band), part_cols]
            for parity in range(2):
                value = result[parity * band : parity * band + band]
                if parity == 0:
                    value = value + shortcut * even
                for frame in range(depth):
                    for k in range(4):
                        m.xs[
                            part_cols.start // 128 + k, frame, row, pl.ds(parity, 8, stride=2), :
                        ] = value[frame * 8 : frame * 8 + 8, k * 128 : k * 128 + 128]

    for part_rows in ((0, 2), (2, 4)):
        pl.loop(*part_rows)(pixel_row)
        for row in range(*part_rows):
            for k, lane in enumerate(lanes):
                store(m.xs.at[k, :, row], m.pixels.at[:, row, :, lane], m.row_sem.at[row])
        if part_rows[0] == 0:
            pump(1)
    for name in ("scaling", "biasing", "amplitudes", "baselines"):
        store(getattr(m, name), getattr(m, name + "_h"))
    pump(None)
    for copy in stores:
        copy.wait()
    for row in range(4):
        wait_row(row)

    @pl.when(below)
    def _():
        pltpu.make_async_remote_copy(
            src_ref=m.a.at[4],
            dst_ref=m.a.at[0],
            send_sem=m.halo_s.at[0],
            recv_sem=m.halo_r.at[0],
            device_id=(f, lax.rem(r + 1, rows)),
            device_id_type=MESH,
        ).wait_send()


def chain(
    x, place_of, length_of, wn, ks, we, wsk, wcr, wer, kst, wex, taps, kern, wce, gain, bias, wide_gain,
    wide_bias, slopes, call,
):
    frames, rows = lax.axis_size("frames"), lax.axis_size("rows")
    depth = x.shape[0]
    band, pad = depth * 8, -(-depth // 16) * 16
    half = 2 * band
    span = band + 16
    levels = int(math.log2(frames // 2))
    b_count = 2 ** (levels // 2)
    a_count = frames // 2 // b_count
    thin = 512 // frames
    blocks = (2, a_count, b_count, thin)
    unit = (a_count, b_count, thin, 512)
    copies = 6 + 2 * (a_count + b_count - 2)
    ring = 3
    hbm, smem = pl.BlockSpec(memory_space=pl.ANY), pl.BlockSpec(memory_space=pltpu.SMEM)

    inputs = dict(
        x=(x, hbm), slope_h=(slopes, hbm), wn_h=(wn, hbm), wsk_h=(wsk, hbm), ks_h=(ks, hbm),
        we_h=(we, hbm), wcr_h=(wcr, hbm), wce_h=(wce, hbm), kern_h=(kern, hbm), wer_h=(wer, hbm),
        kst_h=(kst, hbm), wex_h=(wex, hbm), taps_in_h=(taps, hbm), gain_h=(gain, hbm),
        bias_h=(bias, hbm), wide_gain_h=(wide_gain, hbm), wide_bias_h=(wide_bias, hbm),
        place_of=(place_of, smem), length_of=(length_of, smem),
    )

    def wide_of(*shape):
        return jax.ShapeDtypeStruct(shape, jnp.float32)

    kept = dict(
        xb=(2, 4 * half, 1024), pc=(2, 5, band, 1536), h2=(2, half, 512), uh=(2, half, 2048),
        squashed=(2, half, 512), mixed=(2, 3, 4, band, 384), gc2=(2, half, 2048),
        gk=(2, 3, half, 128), ga2=(2, half, 512),
        gb=(2, 3, band, 1024),
    )
    outputs = dict(
        layer_output=(wide_of(depth, 2, 8, 2048), hbm), pixels=(wide_of(depth, 4, 16, 1024), hbm),
        scaling_h=(wide_of(4, 512), hbm), biasing_h=(wide_of(4, 512), hbm),
        amplitudes_h=(wide_of(3, 2048), hbm), baselines_h=(wide_of(3, 2048), hbm),
        narrower=(wide_of(2, *blocks, 128), hbm), strider=(wide_of(9, *blocks, 128), hbm),
        widener=(wide_of(*blocks, 512), hbm), shortcut=(wide_of(2, *blocks, 512), hbm),
        squeezer=(wide_of(4, *blocks, 128), hbm), restorer=(wide_of(*blocks, 512), hbm),
        pack=(wide_of(2, *blocks, 128), hbm),
    )

    def f32(*shape):
        return pltpu.VMEM(shape, jnp.float32)

    def b16(*shape):
        return pltpu.VMEM(shape, jnp.bfloat16)

    def sems(*shape):
        return pltpu.SemaphoreType.DMA(shape)

    scratch = dict(
        wn=b16(1024, 512), wsk=b16(1024, 2048), ks=b16(3, 1536, 512), we=b16(512, 2048),
        wcr=b16(2048, 512), wce=b16(512, 2048), kern=b16(3, 3, 384, 128),
        xs=f32(8, depth, 4, 16, 128), a=f32(5, 2, band, 512), b=f32(half, 512), c=f32(half, 2048),
        s=f32(half, 2048), d=f32(half, 512), hid=f32(half, 512),
        merged=f32(half, 512), e=f32(half, 2048),
        slope=f32(2, depth, 8, 2048), d2=f32(half, 2048), back=f32(half, 512), eg=f32(half, 512),
        b_halo=f32(band, 512),
        back_halo=f32(band, 512), source=f32(3, 4, span, 128), grad_pad=f32(2, 4, span, 128),
        mixed_grad=f32(2, span, 128), grad_sides=b16(2, 4, span, 384), gate_all=f32(band, 512),
        edge=f32(3, 2, pad, 512), gate=f32(pad, 512),
        gate_part=f32(pad, 512), pooled=f32(pad, 32), follow=f32(pad, 384), tap_in=f32(pad, 384),
        tap_slots=f32(rows, pad, 384), tap_near=f32(rows, 8, 384), gate_slots=f32(rows, pad, 512),
        gate_near=f32(rows, 8, 512), stat=f32(4, 8, 2048), vec=f32(48, 2048), ar_in=f32(2, 48, 128),
        ar_part=f32(2, 48, 128), ar_out=f32(48, 128), ar_rows_a=f32(rows, 32, 128), ar_rows_b=f32(rows, 48, 128),
        ar_frames_a=f32(frames, 32, 128), ar_frames_b=f32(frames, 48, 128), ar_rs=sems(2, rows), ar_rr=sems(2, rows),
        ar_fs=sems(2, max(frames, 16)), ar_fr=sems(2, max(frames, 16)),
        ar_small=f32(2, 16, 8, 128), rows_s=sems(2, 2 * rows),
        rows_r=sems(2, 2 * rows), ring_s=sems(2, 8), ring_r=sems(2, 8), halo_s=sems(3),
        halo_r=sems(3), condenser=f32(32, 512), stencil=f32(32, 384), exciter=f32(32, 512),
        temporal=f32(3, 384), wer=b16(32, 512), kst=b16(288, 32), wex=b16(32, 512),
        taps_in=b16(3, 384), taps=f32(3, 384), gain=f32(4, 512), bias=f32(4, 512),
        wide_gain=f32(3, 2048), wide_bias=f32(3, 2048), before16=f32(pad, 128),
        after16=f32(pad, 128), before_band=f32(band, 128), after_band=f32(band, 128),
        scaling=f32(4, 512), biasing=f32(4, 512), amplitudes=f32(3, 2048), baselines=f32(3, 2048),
        g_own=f32(3, 2, *unit), g_away=f32(3, *unit), g_near=f32(3, 2, *unit),
        g_first_p=f32(ring, b_count - 1, a_count, thin, 512),
        g_first_q=f32(ring, a_count - 1, b_count, thin, 512),
        g_second_p=f32(3, a_count - 1, thin, 512), g_second_q=f32(3, b_count - 1, thin, 512),
        g_third=f32(2, 3, 2, thin, 128), g_fourth=f32(2, 3, thin, 128),
        g_rows=f32(ring, 2, a_count, b_count, thin, 128), g_both=f32(3, a_count, b_count, thin, 128),
        g_first_z=f32(3, a_count - 1, b_count, thin, 128),
        g_second_z=f32(3, b_count - 1, thin, 128),
        g_send=sems(3, ring, copies), g_recv=sems(3, ring, copies),
        load_sem=sems(20), store_sem=sems(8), row_sem=sems(4),
    )
    for name in kept:
        scratch[name] = b16(*kept[name])
    names = list(inputs) + list(outputs) + list(scratch)
    results = pl.pallas_call(
        lambda *refs: chain_kernel(names, (frames, rows, depth, a_count, b_count), *refs),
        out_shape=[shape for shape, _ in outputs.values()],
        in_specs=[spec for _, spec in inputs.values()],
        out_specs=[spec for _, spec in outputs.values()],
        scratch_shapes=list(scratch.values()),
        compiler_params=pltpu.CompilerParams(
            collective_id=call, has_side_effects=True, vmem_limit_bytes=VMEM_BYTES
        ),
    )(*[value for value, _ in inputs.values()])
    return SimpleNamespace(**dict(zip(outputs, results)))


def finish_kernel(count, *refs):
    pack, refs = refs[0], refs[1:]
    sources, refs = refs[:count], refs[count:]
    targets, refs = refs[:count], refs[count:]
    condenser, stencil, exciter, temporal, kernels, tail = refs[:6]
    held, in_sems, out_sems = refs[6:-2], refs[-2], refs[-1]
    first = [
        pltpu.make_async_copy(source, block, in_sems.at[k])
        for k, (source, block) in enumerate(zip(sources, held))
    ]
    first.append(pltpu.make_async_copy(pack, tail, in_sems.at[count]))
    for copy in first:
        copy.start()
    second = []

    def put_out(source, target):
        copy = pltpu.make_async_copy(source, target, out_sems.at[len(second)])
        copy.start()
        second.append(copy)

    for copy, block, target in zip(first, held, targets):
        copy.wait()
        put_out(block, target)
    first[-1].wait()
    for tap in range(27):
        kernels[tap] = tail[tap * 32 : tap * 32 + 32, :]
    for q in range(4):
        condenser[:, q * 128 : q * 128 + 128] = tail[864 + q * 8 : 872 + q * 8, :]
    exciter[...] = tail[928:960, :]
    for tap in range(9):
        start, lane = 896 + tap // 4 * 8, tap % 4 * 32
        stencil[tap] = tail[start : start + 8, lane : lane + 32]
    temporal[...] = tail[920:923, :96]
    for copy in second:
        copy.wait()


def finish(pack, arrays):
    hbm, vmem = pl.BlockSpec(memory_space=pl.ANY), pl.BlockSpec(memory_space=pltpu.VMEM)
    shapes = [array.shape for array in arrays]
    shapes += [(8, 512), (9, 8, 32), (32, 128), (3, 96), (27, 32, 128)]
    count = len(arrays)
    return pl.pallas_call(
        lambda *refs: finish_kernel(count, *refs),
        out_shape=[jax.ShapeDtypeStruct(shape, jnp.float32) for shape in shapes],
        in_specs=[hbm] * (count + 1),
        out_specs=[hbm] * count + [vmem] * 5,
        scratch_shapes=[
            pltpu.VMEM(shape, jnp.float32) for shape in [pack.shape, *shapes[:count]]
        ]
        + [pltpu.SemaphoreType.DMA((count + 1,)), pltpu.SemaphoreType.DMA((count,))],
        compiler_params=pltpu.CompilerParams(vmem_limit_bytes=VMEM_BYTES),
    )(pack, *arrays)


def shards(
    input_feature_maps,
    sequence_slot_lookup,
    sequence_span_lookup,
    opening_reducer,
    downsampling_filter,
    opening_expander,
    skip_projection,
    closing_reducer,
    excite_reducer,
    excite_spatial_filter,
    excite_expander,
    time_taps,
    spatial_filters,
    closing_expander,
    narrow_norm_gains,
    narrow_norm_biases,
    wide_norm_gains,
    wide_norm_biases,
    loss_slope_wrt_final,
):
    k = chain(
        input_feature_maps,
        sequence_slot_lookup,
        sequence_span_lookup,
        opening_reducer,
        downsampling_filter.reshape(3, 1536, 512),
        opening_expander,
        skip_projection,
        closing_reducer,
        excite_reducer.T,
        excite_spatial_filter.reshape(288, 32),
        excite_expander,
        time_taps,
        spatial_filters.reshape(3, 3, 384, 128),
        closing_expander,
        narrow_norm_gains,
        narrow_norm_biases,
        wide_norm_gains,
        wide_norm_biases,
        loss_slope_wrt_final,
        0,
    )
    results = finish(
        k.pack.reshape(-1, 128),
        (
            k.layer_output,
            k.pixels,
            k.narrower.reshape(opening_reducer.shape[0], -1),
            k.strider.reshape(downsampling_filter.shape[:-1] + (-1,)),
            k.widener.reshape(opening_expander.shape[0], -1),
            k.shortcut.reshape(skip_projection.shape[0], -1),
            k.squeezer.reshape(closing_reducer.shape[0], -1),
            k.restorer.reshape(closing_expander.shape[0], -1),
            k.scaling_h,
            k.biasing_h,
            k.amplitudes_h,
            k.baselines_h,
        ),
    )
    condenser, stencil, exciter, temporal, kernels = results[12:]
    return (
        *results[:7],
        condenser.T,
        stencil.transpose(0, 2, 1).reshape(excite_spatial_filter.shape[:-1] + (-1,)),
        exciter,
        temporal,
        kernels.transpose(0, 2, 1).reshape(spatial_filters.shape[:-1] + (-1,)),
        *results[7:12],
    )


def solution(mesh):
    return jax.shard_map(
        shards,
        mesh=mesh,
        in_specs=(
            P("frames", "rows", None, None),
            P("frames"),
            P("frames"),
            P(),
            P(),
            P(),
            P(),
            P(),
            P(),
            P(),
            P(),
            P(),
            P(),
            P(),
            P(),
            P(),
            P(),
            P(),
            P("frames", "rows", None, None),
        ),
        out_specs=(
            P("frames", "rows", None, None),
            P("frames", "rows", None, None),
            P(None, "rows"),
            P(None, None, None, "rows"),
            P(None, "rows"),
            P(None, "rows"),
            P(None, "rows"),
            P(None, "rows"),
            P(None, None, None, "rows"),
            P(None, "rows"),
            P(None, "rows"),
            P(None, None, None, None, "rows"),
            P(None, "rows"),
            P(),
            P(),
            P(),
            P(),
        ),
        check_vma=False,
    )
```

profile of v0, /device:TPU:0, one launch (start us, length us, event | category | flops | bytes accessed | tf_op | source)
XLA Modules:
  0.0 314.4 jit_solution(9840510729404970854)
XLA Ops:
  0.7 303.2 %shard_map.314 = (f32[12,2,8,2048]{3,2,1,0:T(8,128)}, f32[12,4,16,1024]{3,2,1,0:T(8,128)}, f32[4,512]{1,0:T(4,128)}, f32[4,512]{1,0:T(4,128)}, f32[3,2048]{1,0:T...) custom-call(f32[12,4,16,1024]{3,2,1,0:T(8,128)} %refs_0_.1, ...), custom_call_target="tpu_custom_call" | custom-call | tf_op jit(solution)/shard_map/pallas_call | solution.py:1510
  303.9 10.3 %shard_map.315 = (f32[12,2,8,2048]{3,2,1,0:T(8,128)}, f32[12,4,16,1024]{3,2,1,0:T(8,128)}, f32[1024,128]{1,0:T(8,128)}, f32[3,3,512,128]{3,2,1,0:T(8,128)}, f32[...) custom-call(f32[1024,128]{1,0:T(8,128)} %bitcast.26, ...), custom_call_target="tpu_custom_call" | custom-call | tf_op jit(solution)/shard_map/pallas_call | solution.py:1565
where the time goes:
time: 319 us; the launch traced here: 314 us
  Pallas kernels  314 us (98%)
    pallas_call x1, Pallas kernels, chain(): pl.pallas_call(lambda *refs: chain_kernel(names, (frames, rows, depth, a_...  303 us
    pallas_call x1, Pallas kernels, finish(): pl.pallas_call(lambda *refs: finish_kernel(count, *refs), out_shape=[jax....  10.3 us

commit v1 on v0

--- a/solution.py
+++ b/solution.py
@@ -398,7 +398,7 @@
             yield from over_b(lambda i: first.at[0, i], second, ())
             final = second.at[0]
         orders = ((b_count, b_peer), (a_count, a_peer))
-        (one_count, one_peer), (two_count, two_peer) = orders[:: 1 if kind % 2 == 0 else -1]
+        (one_count, one_peer), (two_count, two_peer) = orders[:: 1 if kind == 0 else -1]
         local = pltpu.make_async_copy(final, out.at[c, ia, ib], bank[1].at[used[0]])
         used[0] += 1
         local.start()
@@ -410,7 +410,7 @@
         local.wait()
         done(copies)
         copies = []
-        field = out.at[c, ia] if kind % 2 == 0 else out.at[c, :, ib]
+        field = out.at[c, ia] if kind == 0 else out.at[c, :, ib]
         for step in range(1, two_count):
             _, device = two_peer(step)
             copies.append(go(field, field, device))

time: 319 us -> 319 us (level)
  no operation moved by 1% of the time
where the time goes in v1:
time: 319 us; the launch traced here: 314 us
  Pallas kernels  313 us (98%)
    pallas_call x1, Pallas kernels, chain(): pl.pallas_call(lambda *refs: chain_kernel(names, (frames, rows, depth, a_...  303 us
    pallas_call x1, Pallas kernels, finish(): pl.pallas_call(lambda *refs: finish_kernel(count, *refs), out_shape=[jax....  10.3 us

profile of v1, /device:TPU:0, one launch (start us, length us, event | category | flops | bytes accessed | tf_op | source)
XLA Modules:
  0.0 313.9 jit_solution(13746620293438982980)
XLA Ops:
  0.7 302.7 %shard_map.314 = (f32[12,2,8,2048]{3,2,1,0:T(8,128)}, f32[12,4,16,1024]{3,2,1,0:T(8,128)}, f32[4,512]{1,0:T(4,128)}, f32[4,512]{1,0:T(4,128)}, f32[3,2048]{1,0:T...) custom-call(f32[12,4,16,1024]{3,2,1,0:T(8,128)} %refs_0_.1, ...), custom_call_target="tpu_custom_call" | custom-call | tf_op jit(solution)/shard_map/pallas_call | solution.py:1510
  303.4 10.3 %shard_map.315 = (f32[12,2,8,2048]{3,2,1,0:T(8,128)}, f32[12,4,16,1024]{3,2,1,0:T(8,128)}, f32[1024,128]{1,0:T(8,128)}, f32[3,3,512,128]{3,2,1,0:T(8,128)}, f32[...) custom-call(f32[1024,128]{1,0:T(8,128)} %bitcast.26, ...), custom_call_target="tpu_custom_call" | custom-call | tf_op jit(solution)/shard_map/pallas_call | solution.py:1565
